TPU v7x, 512 devices: a whole 4x8x8 slice. The times are simulated.
512 devices in a mesh: leaf: 8 (over y), row: 8 (over z_hi, x), col: 8 (over z_lo, core).
Axes of the slice: x: 4, y: 8, z: 8 (z_hi: 2, z_lo: 4; z = z_hi * 4 + z_lo), core: 2. Of those that a mesh axis runs over, the one named last changes fastest.
Arguments:
- parent_front: float32 [2, 1, 8192, 8, 1024], P(None, None, ('leaf', 'row'), None, 'col'), as said below
- child_updates: float32 [2, 1, 8192, 4, 1024], P(None, None, ('leaf', 'row'), None, 'col')
- child_map: int32 [2, 32], replicated, may hold values from 0 to 63, as said below
Outputs:
- factored_front: float32 [2, 1, 8192, 8, 1024], P(None, None, ('leaf', 'row'), None, 'col')
Inputs may be any that keep to these rules, and one draw needn't show every extreme that they name: For each child c the entries child_map[c, :] are distinct, child_map[c, a] leaves the same remainder modulo 8 as a, and each child's map contains the first and the last parent block of every remainder class. Each row of the parent front's pivot block has a diagonal entry whose magnitude exceeds the norm of the row's other entries in that block; parent_front and child_updates are complex symmetric.
All inputs are finite; a program needn't handle non-finite values.
Results may differ from a plain program's by a relative error of at most 0.0015.
Values may be sent and summed in bfloat16 or wider, within the bound.
No kernel may reach another device: no remote copies, remote signals or barrier semaphores. Data moves between devices by JAX's collectives and lax.ppermute only.
A program may use at most 64 MiB of HBM per device.

v0:
```python
import jax
import jax.numpy as jnp
from jax import lax
from jax.sharding import PartitionSpec as P

NS_STEPS = 3


def spread(value, axis, source):
    kept = jnp.where(lax.axis_index(axis) == source, value, 0).astype(value.dtype)
    return lax.psum(kept, axis)


def complex_product(left, right):
    real_part = jnp.matmul(left[0], right[0], precision=lax.Precision.HIGHEST) - jnp.matmul(
        left[1], right[1], precision=lax.Precision.HIGHEST
    )
    imag_part = jnp.matmul(left[0], right[1], precision=lax.Precision.HIGHEST) + jnp.matmul(
        left[1], right[0], precision=lax.Precision.HIGHEST
    )
    return jnp.stack([real_part, imag_part])


def transposed_product(left, right):
    real_part = jnp.einsum(
        "rp,cp->rc", left[0], right[0], preferred_element_type=jnp.float32
    ) - jnp.einsum("rp,cp->rc", left[1], right[1], preferred_element_type=jnp.float32)
    imag_part = jnp.einsum(
        "rp,cp->rc", left[0], right[1], preferred_element_type=jnp.float32
    ) + jnp.einsum("rp,cp->rc", left[1], right[0], preferred_element_type=jnp.float32)
    return jnp.stack([real_part, imag_part])


def newton_inverse(pivot_block):
    diag_real = jnp.diagonal(pivot_block[0])
    diag_imag = jnp.diagonal(pivot_block[1])
    denominator = diag_real * diag_real + diag_imag * diag_imag
    current = jnp.stack([jnp.diag(diag_real / denominator), jnp.diag(-diag_imag / denominator)])
    for newton_step in range(NS_STEPS):
        product = complex_product(pivot_block, current)
        current = 2.0 * current - complex_product(current, product)
    return current


def local(parent_front, child_updates, child_map):
    leaf_count = lax.axis_size("leaf")
    row_count = lax.axis_size("row")
    col_count = lax.axis_size("col")
    rank_count = leaf_count * row_count
    half_ranks = rank_count // 2
    my_row = lax.axis_index("row")
    my_col = lax.axis_index("col")
    my_rank = lax.axis_index("leaf") * row_count + my_row
    row_blocks = parent_front.shape[1]
    block_size = parent_front.shape[2]
    local_cols = parent_front.shape[3]
    child_rows = child_updates.shape[1]
    child_cols = child_updates.shape[3]
    child_order = child_map.shape[1]
    panel_width = 2 * block_size
    flat_map = child_map.reshape(-1)
    pieces = lax.all_gather(child_updates[None], "leaf", axis=0, tiled=True)
    senders = pieces.shape[0]
    source_leaf = jnp.arange(senders, dtype=jnp.int32)
    source_rank = source_leaf * row_count + my_row
    source_child = source_rank // half_ranks
    source_slot = source_rank % half_ranks
    child_block = (
        jnp.arange(child_rows, dtype=jnp.int32)[None, :] * half_ranks + source_slot[:, None]
    )
    target_rows = jnp.take(flat_map, source_child[:, None] * child_order + child_block)
    local_index = jnp.arange(row_blocks, dtype=jnp.int32)
    row_select = (
        (target_rows[:, :, None] % rank_count == my_rank)
        & (target_rows[:, :, None] // rank_count == local_index[None, None, :])
    ).astype(jnp.float32)
    column_block = jnp.arange(child_cols, dtype=jnp.int32) * col_count + my_col
    target_cols = jnp.take(flat_map, source_child[:, None] * child_order + column_block[None, :])
    col_select = (
        target_cols[:, :, None] // col_count
        == jnp.arange(local_cols, dtype=jnp.int32)[None, None, :]
    ).astype(jnp.float32)
    added = jnp.einsum(
        "ntu,nztxby,nbs->zuxsy", row_select, pieces, col_select, precision=lax.Precision.HIGHEST
    )
    assembled = parent_front + added
    first_block = assembled[:, :, :, 0, :]
    columns = [spread(first_block, "col", owner) for owner in range(2)]
    panel_rows = jnp.concatenate(columns, axis=3)
    pivot_parts = [
        spread(panel_rows[:, 0].astype(jnp.bfloat16), ("leaf", "row"), owner).astype(jnp.float32)
        for owner in range(2)
    ]
    pivot_block = jnp.concatenate(pivot_parts, axis=1)
    inverse = newton_inverse(pivot_block)
    multipliers = complex_product(
        panel_rows.reshape(2, row_blocks * block_size, panel_width), inverse
    )
    compact = panel_rows.astype(jnp.bfloat16)
    gathered = lax.all_gather(compact, ("leaf", "row"), axis=2, tiled=True)
    gathered = gathered.reshape(
        2, row_blocks, rank_count // col_count, col_count, block_size, panel_width
    )
    gathered = lax.dynamic_index_in_dim(gathered, my_col, axis=3, keepdims=False)
    column_panel = gathered.reshape(2, local_cols * block_size, panel_width)
    update_all = transposed_product(multipliers.astype(jnp.bfloat16), column_panel)
    schur_part = assembled - update_all.reshape(assembled.shape)
    column_start = jnp.minimum(my_col, 1) * block_size
    mult_piece = lax.dynamic_slice_in_dim(multipliers, column_start, block_size, axis=2)
    mult_piece = mult_piece.reshape(2, row_blocks, block_size, 1, block_size)
    global_row = jnp.arange(row_blocks, dtype=jnp.int32) * rank_count + my_rank
    global_col = jnp.arange(local_cols, dtype=jnp.int32) * col_count + my_col
    pivot_row = (global_row < 2)[None, :, None, None, None]
    panel_col = (global_col < 2)[None, None, None, :, None]
    return jnp.where(pivot_row, assembled, jnp.where(panel_col, mult_piece, schur_part))


def solution(mesh):
    in_specs = (
        P(None, None, ("leaf", "row"), None, "col"),
        P(None, None, ("leaf", "row"), None, "col"),
        P(),
    )
    out_specs = P(None, None, ("leaf", "row"), None, "col")
    return jax.shard_map(local, mesh=mesh, in_specs=in_specs, out_specs=out_specs, check_vma=False)
```

profile of v0, /device:TPU:2, one launch (start us, length us, event | category | flops | bytes accessed | tf_op | source)
XLA Modules:
  0.0 1166.9 jit_solution(15491226585552927433)
XLA Ops:
  6.5 2.0 copy.17
  8.8 0.8 reshape.505
  9.6 0.7 gather_fusion
  10.5 0.7 gather_fusion.1
  11.2 60.0 %all-gather.6.cloned.1.call-done = f32[16,1,128,4,128]{4,2,3,1,0:T(8,128)} async-done(((f32[2,1,128,4,128]{4,2,3,1,0:T(8,128)}), f32[16,1,128,4,128]{4,2,3,1,0:T(8,128)}) %all-gather.6.cloned.1.call-update) | async-done | bytes 4194320 | tf_op jit(solution)/shard_map/all_gather | solution.py:62
  71.2 11.3 fusion.5
  82.6 0.8 broadcast_select_fusion
  83.4 0.7 select_bitcast_fusion.2
  84.1 75.9 %all-reduce.5.cloned.1.call-done = (f32[2,1,128,128]{3,2,0,1:T(8,128)}, f32[2,1,128,128]{3,2,0,1:T(8,128)}) async-done(((f32[2,1,128,128]{3,2,0,1:T(8,128)}, f32[2,1,128,128]{3,2,0,1:T(8,128)}), (f32[2,1,128,128]{3,2,0,1:T(8,128)}, f32[2,1,128,128]{3,2,0,1:T(8,128)})) %all-reduce.5.cloned.1.call-update) | async-done | bytes 262160 | tf_op jit(solution)/shard_map/psum | solution.py:11
  160.0 0.9 constant_dynamic-update-slice_fusion.1
  161.0 0.9 constant_dynamic-update-slice_fusion
  161.9 0.7 select_bitcast_fusion
  162.6 0.7 select_bitcast_fusion.1
  163.5 0.3 all-gather.4.cloned.1.call-update
  163.9 785.1 %all-reduce.7.cloned.1.call-done = (bf16[2,128,256]{2,1,0:T(8,128)(2,1)}, bf16[2,128,256]{2,1,0:T(8,128)(2,1)}) async-done(((bf16[2,128,256]{2,1,0:T(8,128)(2,1)}, bf16[2,128,256]{2,1,0:T(8,128)(2,1)}), (bf16[2,128,256]{2,1,0:T(8,128)(2,1)}, bf16[2,128,256]{2,1,0:T(8,128)(2,1)})) %all-reduce.7.cloned.1.call-update) | async-done | bytes 262160 | tf_op jit(solution)/shard_map/psum | solution.py:11
  949.0 0.9 constant_dynamic-update-slice_fusion.3
  949.9 0.9 constant_dynamic-update-slice_fusion.2
  951.0 2.3 gather_fusion.2
  953.3 2.3 gather_fusion.3
  955.7 0.3 fusion.32
  956.0 0.4 fusion.24
  956.4 0.3 convolution_subtract_fusion.6
  956.7 0.4 fusion.30
  957.2 0.3 convolution_add_fusion.6
  957.5 0.4 fusion.15
  957.9 0.4 fusion.27
  958.4 0.4 fusion.14
  959.1 0.3 fusion.41
  959.7 0.3 convolution_subtract_fusion.4
  960.0 0.4 fusion.40
  960.4 0.3 convolution_add_fusion.4
  960.7 0.4 fusion.13
  961.1 0.4 fusion.39
  961.5 0.4 fusion.12
  962.0 0.3 fusion.45
  962.3 0.3 fusion.46
  962.6 0.3 convolution_subtract_fusion.2
  962.9 0.4 fusion.44
  963.3 0.3 convolution_add_fusion.2
  963.6 0.4 fusion.11
  964.0 0.4 fusion.43
  964.4 0.4 fusion.10
  966.1 190.3 %all-gather.4.cloned.1.call-done = bf16[2,1,8192,256]{3,2,0,1:T(8,128)(2,1)} async-done(((bf16[2,1,128,256]{3,2,0,1:T(8,128)(2,1)}), bf16[2,1,8192,256]{3,2,0,1:T(8,128)(2,1)}) %all-gather.4.cloned.1.call-update) | async-done | bytes 8388624 | tf_op jit(solution)/shard_map/all_gather | solution.py:100
  1156.4 1.3 constant_dynamic-slice_fusion
  1158.0 0.3 fusion.64
  1158.3 0.3 fusion.9
  1158.7 0.3 fusion.8
  1159.1 1.2 fusion.20
  (42 shorter events, 3.4 us)
Async XLA Ops:
  6.5 64.7 %copy-start.1 = (f32[2,1,128,8,128]{4,3,2,1,0:T(8,128)S(1)}, f32[2,1,128,8,128]{4,3,2,1,0:T(8,128)}, u32[]{:S(2)}) copy-start(f32[2,1,128,8,128]{4,3,2,1,0:T(8,128)} %param.3) | copy-start | bytes 3145732
  6.5 64.7 %all-gather.6.cloned.1.call-start = ((), (), s32[]{:S(2)}) async-start(), calls=%async_computation.1 | async-start | bytes 4718592 | tf_op jit(solution)/shard_map/all_gather | solution.py:62
  8.5 151.5 %all-reduce.5.cloned.1.call-start = ((), (), s32[]{:S(2)}) async-start(), calls=%async_computation.2 | async-start | bytes 524288 | tf_op jit(solution)/shard_map/psum | solution.py:11
  84.1 864.9 %all-reduce.7.cloned.1.call-start = ((), (), s32[]{:S(2)}) async-start(), calls=%async_computation.3 | async-start | bytes 524288 | tf_op jit(solution)/shard_map/psum | solution.py:11
  162.5 1.0 copy-start
  163.3 993.1 %all-gather.4.cloned.1.call-start = ((), (), s32[]{:S(2)}) async-start(), calls=%async_computation | async-start | bytes 8519680 | tf_op jit(solution)/shard_map/all_gather | solution.py:100
Sparse Core Ops, SparseCore 0:
  9.4 61.7 all-gather.5
  84.2 75.7 all-reduce.4
  163.4 785.5 all-reduce.6
  953.3 203.0 all-gather.3
where the time goes:
time: 1170 us
  waiting for transfers between devices  1110 us (95%)
  matrix products  22.2 us (2%)
  local copies, waits for them, and re-layouts  14.2 us (1%)
  between operations  13.6 us (1%)
    psum x2, waiting for transfers between devices, spread(): return lax.psum(kept, axis)  861 us
    all_gather x1, waiting for transfers between devices, local(): gathered = lax.all_gather(compact, ('leaf', 'row'), axis=2, tiled=True)  190 us
    all_gather x1, waiting for transfers between devices, local(): pieces = lax.all_gather(child_updates[None], 'leaf', axis=0, tiled=True)  60 us
  transfers between devices with their start and end apart: 4, of which 4 were waited for; matrix products, arithmetic and copies ran while one was open for 2% of the time, Pallas kernels for 0%

commit v1 on v0

--- a/solution.py
+++ b/solution.py
@@ -8,7 +8,7 @@
 
 def spread(value, axis, source):
     kept = jnp.where(lax.axis_index(axis) == source, value, 0).astype(value.dtype)
-    return lax.psum(kept, axis)
+    return jnp.sum(lax.all_gather(kept, axis), axis=0)
 
 
 def complex_product(left, right):

time: 1170 us -> 778 us (0.66)
  waiting for transfers between devices: 1110 us -> 715 us
    psum x2 -> x0, waiting for transfers between devices: 861 us -> none  [spread(): return lax.psum(kept, axis)]
    all_gather x0 -> x4, waiting for transfers between devices: none -> 473 us  [spread(): return jnp.sum(lax.all_gather(kept, axis), axis=0)]
    reduce_sum x0 -> x4, other arithmetic: none -> 11.7 us  [spread(): return jnp.sum(lax.all_gather(kept, axis), axis=0)]
  transfers between devices with their start and end apart: 4 -> 6, of which waited for: 4 -> 6; matrix products, arithmetic and copies ran while one was open for 2% -> 4% of each run, Pallas kernels for 0% -> 0%
where the time goes in v1:
time: 778 us
  waiting for transfers between devices  715 us (92%)
  matrix products  22.2 us (3%)
  other arithmetic  16 us (2%)
  between operations  13.9 us (2%)
  local copies, waits for them, and re-layouts  10.4 us (1%)
    all_gather x4, waiting for transfers between devices, spread(): return jnp.sum(lax.all_gather(kept, axis), axis=0)  473 us
    all_gather x1, waiting for transfers between devices, local(): gathered = lax.all_gather(compact, ('leaf', 'row'), axis=2, tiled=True)  181 us
    all_gather x1, waiting for transfers between devices, local(): pieces = lax.all_gather(child_updates[None], 'leaf', axis=0, tiled=True)  60.1 us
  transfers between devices with their start and end apart: 6, of which 6 were waited for; matrix products, arithmetic and copies ran while one was open for 4% of the time, Pallas kernels for 0%

profile of v1, /device:TPU:2, one launch (start us, length us, event | category | flops | bytes accessed | tf_op | source)
XLA Modules:
  0.0 777.8 jit_solution(18082903246671114510)
XLA Ops:
  6.5 1.9 copy.13
  8.7 0.8 reshape.537
  9.4 0.7 gather_fusion
  10.4 0.6 gather_fusion.1
  11.1 60.1 %all-gather.14.cloned.1.call-done = f32[16,1,128,4,128]{4,2,3,1,0:T(8,128)} async-done(((f32[2,1,128,4,128]{4,2,3,1,0:T(8,128)}), f32[16,1,128,4,128]{4,2,3,1,0:T(8,128)}) %all-gather.14.cloned.1.call-update) | async-done | bytes 4194320 | tf_op jit(solution)/shard_map/all_gather | solution.py:62
  71.2 11.3 %fusion.5 = f32[2,1,128,8,128]{4,3,2,0,1:T(8,128)S(1)} fusion(f32[8,2,128,4,128]{4,2,3,1,0:T(8,128)} %bitcast.166, f32[2,1,128,8,128]{4,3,2,1,0:T(8,128)} %param.3, f32[8]{0:T(128)S(1)} %and_convert_fusion, s32[8,4]{0,1:T(4,128)S(1)} %copy.12), kind=kOutput, calls=%fused_computation.9 | convolution fusion | flops 100925952 | bytes 6291616 | tf_op jit(solution)/shard_map/ntu,nztxby,nbs->zuxsy/dot_general | solution.py:83
  82.5 0.9 broadcast_select_fusion.1
  83.5 0.7 all-gather.18.cloned.1.call-update
  84.2 38.7 %all-gather.16.cloned.1.call-done = f32[16,1,128,1,128]{4,2,3,1,0:T(8,128)} async-done(((f32[2,1,128,1,128]{4,2,3,1,0:T(8,128)}), f32[16,1,128,1,128]{4,2,3,1,0:T(8,128)}) %all-gather.16.cloned.1.call-update) | async-done | bytes 1048592 | tf_op jit(solution)/shard_map/all_gather | solution.py:11
  122.9 1.3 reduce.4
  124.2 39.9 %all-gather.18.cloned.1.call-done = f32[16,1,128,1,128]{4,2,3,1,0:T(8,128)} async-done(((f32[2,1,128,1,128]{4,2,3,1,0:T(8,128)}), f32[16,1,128,1,128]{4,2,3,1,0:T(8,128)}) %all-gather.18.cloned.1.call-update) | async-done | bytes 1048592 | tf_op jit(solution)/shard_map/all_gather | solution.py:11
  164.2 1.3 reduce.5
  165.5 0.7 broadcast_select_fusion.2
  166.1 0.7 broadcast_select_fusion.3
  166.9 0.5 all-gather.22.cloned.1.call-update
  167.7 0.3 all-gather.12.cloned.1.call-update
  168.1 199.6 %all-gather.20.cloned.1.call-done = bf16[128,1,128,256]{3,2,1,0:T(8,128)(2,1)} async-done(((bf16[2,1,128,256]{3,2,1,0:T(8,128)(2,1)}), bf16[128,1,128,256]{3,2,1,0:T(8,128)(2,1)}) %all-gather.20.cloned.1.call-update) | async-done | bytes 8388624 | tf_op jit(solution)/shard_map/all_gather | solution.py:11
  367.6 4.6 bitcast_reduce_fusion.1
  372.2 194.3 %all-gather.22.cloned.1.call-done = bf16[128,1,128,256]{3,2,1,0:T(8,128)(2,1)} async-done(((bf16[2,1,128,256]{3,2,1,0:T(8,128)(2,1)}), bf16[128,1,128,256]{3,2,1,0:T(8,128)(2,1)}) %all-gather.22.cloned.1.call-update) | async-done | bytes 8388624 | tf_op jit(solution)/shard_map/all_gather | solution.py:11
  566.6 4.6 bitcast_reduce_fusion
  571.2 2.3 gather_fusion.2
  573.6 2.3 gather_fusion.3
  576.0 0.3 fusion.32
  576.3 0.3 fusion.24
  576.7 0.4 convolution_subtract_fusion.6
  577.0 0.4 fusion.30
  577.5 0.3 convolution_add_fusion.6
  577.8 0.4 fusion.15
  578.2 0.4 fusion.27
  578.7 0.4 fusion.14
  580.2 0.4 fusion.42
  580.6 0.3 convolution_add_fusion.4
  580.9 0.4 fusion.13
  581.3 0.4 fusion.41
  581.7 0.4 fusion.12
  582.8 0.3 convolution_subtract_fusion.2
  583.1 0.4 fusion.46
  583.5 0.3 convolution_add_fusion.2
  583.8 0.4 fusion.11
  584.2 0.4 fusion.45
  584.6 0.4 fusion.10
  586.4 180.6 %all-gather.12.cloned.1.call-done = bf16[2,1,8192,256]{3,2,1,0:T(8,128)(2,1)} async-done(((bf16[2,1,128,256]{3,2,1,0:T(8,128)(2,1)}), bf16[2,1,8192,256]{3,2,1,0:T(8,128)(2,1)}) %all-gather.12.cloned.1.call-update) | async-done | bytes 8388624 | tf_op jit(solution)/shard_map/all_gather | solution.py:100
  767.0 1.3 constant_dynamic-slice_fusion
  768.2 0.3 fusion.75
  768.5 0.3 fusion.74
  768.9 0.3 fusion.9
  769.3 0.3 fusion.8
  769.7 1.2 fusion.20
  (45 shorter events, 4.3 us)
Async XLA Ops:
  6.5 64.7 %all-gather.14.cloned.1.call-start = ((), (), s32[]{:S(2)}) async-start(), calls=%async_computation.1 | async-start | bytes 4718592 | tf_op jit(solution)/shard_map/all_gather | solution.py:62
  8.4 114.5 %all-gather.16.cloned.1.call-start = ((), (), s32[]{:S(2)}) async-start(), calls=%async_computation.2 | async-start | bytes 1179648 | tf_op jit(solution)/shard_map/all_gather | solution.py:11
  83.4 80.8 %all-gather.18.cloned.1.call-start = ((), (), s32[]{:S(2)}) async-start(), calls=%async_computation.3 | async-start | bytes 1179648 | tf_op jit(solution)/shard_map/all_gather | solution.py:11
  84.1 283.5 %all-gather.20.cloned.1.call-start = ((), (), s32[]{:S(2)}) async-start(), calls=%async_computation.4 | async-start | bytes 8519680 | tf_op jit(solution)/shard_map/all_gather | solution.py:11
  166.1 1.6 copy-start
  166.9 399.7 %all-gather.22.cloned.1.call-start = ((), (), s32[]{:S(2)}) async-start(), calls=%async_computation.5 | async-start | bytes 8519680 | tf_op jit(solution)/shard_map/all_gather | solution.py:11
  167.5 599.5 %all-gather.12.cloned.1.call-start = ((), (), s32[]{:S(2)}) async-start(), calls=%async_computation | async-start | bytes 8519680 | tf_op jit(solution)/shard_map/all_gather | solution.py:100
Sparse Core Ops, SparseCore 0:
  9.4 61.7 all-gather.13
  83.5 39.3 all-gather.15
  125.0 39.0 all-gather.17
  168.5 199.0 all-gather.19
  372.0 194.5 all-gather.21
  570.8 196.1 all-gather.11
